TPU v7x, 32 devices: a whole 2x2x4 slice. The times are simulated.
32 devices in a mesh: seq: 4 (over x, core), head: 4 (over z), batch: 2 (over y).
Axes of the slice: x: 2, y: 2, z: 4, core: 2. Of those that a mesh axis runs over, the one named last changes fastest.
Arguments:
- hyena_inputs: bfloat16 [4096, 3, 8192], P(('batch', 'seq'), None, 'head'), parts along dimension 0, may hold values from -6 to 6
- short_filter: float32 [3, 3, 8192], P(None, None, 'head'), may hold values from -3.5 to 3.5
- medium_filter: float32 [128, 8192], P(None, 'head'), may hold values from -0.5 to 0.5
- q_proj: bfloat16 [4096, 8192], P(('batch', 'seq'), 'head'), parts along dimension 0, may hold values from -8 to 8
- k_proj: bfloat16 [4096, 8192], P(('batch', 'seq'), 'head'), parts along dimension 0, may hold values from -8 to 8
- out_weight: bfloat16 [8192, 8192], P('head'), may hold values from -0.25 to 0.25
Outputs:
- hyena_out: bfloat16 [4096, 8192], P(('batch', 'seq'), 'head'), parts along dimension 0
- mixed: bfloat16 [4096, 8192], P(('batch', 'seq'), 'head'), parts along dimension 0
There are 2 independent parts, one for each index of `batch`. A program takes and returns all parts, laid end to end along the dimension named above; an argument that names none is the same for every part. Nothing has to cross between parts.
All inputs are finite; a program needn't handle non-finite values.
Results may differ from a plain program's by a relative error of at most 0.011.
Values may be sent and summed in bfloat16 or wider, within the bound.
A program may use at most 192 MiB of HBM per device.

v0:
```python
import math
import jax
import jax.numpy as jnp
from jax import lax
from jax.sharding import PartitionSpec as P

HEAD_SIZE = 128


def passed_along(x, axis, by):
    length = lax.axis_size(axis)
    pairs = [(i, i + by) for i in range(length) if 0 <= i + by < length]
    return lax.ppermute(x, axis, pairs)


def causal_depthwise(extended, taps, out_rows):
    tap_count = taps.shape[0]
    window = extended[extended.shape[0] - out_rows - tap_count + 1 :]
    kernel = taps[::-1][:, None, :]
    result = lax.conv_general_dilated(
        window[None],
        kernel,
        (1,),
        "VALID",
        feature_group_count=extended.shape[1],
        dimension_numbers=("NWC", "WIO", "NWC"),
        precision=lax.Precision.HIGHEST,
    )
    return result[0]


def per_device(hyena_inputs, short_filter, medium_filter, q_proj, k_proj, out_weight):
    tok_rows = hyena_inputs.shape[0]
    chan_width = hyena_inputs.shape[2]
    short_taps = short_filter.shape[1]
    med_taps = medium_filter.shape[0]
    short_table = jnp.transpose(short_filter, (1, 0, 2)).reshape(short_taps, 3 * chan_width)
    input_margin = passed_along(hyena_inputs[tok_rows - (short_taps - 1) :], "seq", 1)
    joined = (
        jnp.concatenate([input_margin, hyena_inputs], 0)
        .astype(jnp.float32)
        .reshape(-1, 3 * chan_width)
    )
    filtered = causal_depthwise(joined, short_table, tok_rows).reshape(tok_rows, 3, chan_width)
    product = (filtered[:, 1] * filtered[:, 2]).astype(jnp.bfloat16)
    product_margin = passed_along(product[tok_rows - (med_taps - 1) :], "seq", 1)
    product_ext = jnp.concatenate([product_margin, product], 0)
    medium = causal_depthwise(product_ext.astype(jnp.float32), medium_filter, tok_rows)
    hyena_out = (filtered[:, 0] * medium).astype(jnp.bfloat16)
    head_count = chan_width // HEAD_SIZE
    score_scale = HEAD_SIZE ** (-0.5)
    seq_index = lax.axis_index("seq")
    queries = q_proj.reshape(tok_rows, head_count, HEAD_SIZE)
    query_pos = seq_index * tok_rows + jnp.arange(tok_rows, dtype=jnp.int32)
    last_query = seq_index * tok_rows + tok_rows - 1
    initial = (
        jnp.zeros((head_count, tok_rows, HEAD_SIZE), jnp.float32),
        jnp.full((head_count, tok_rows), -1e30, jnp.float32),
        jnp.zeros((head_count, tok_rows), jnp.float32),
    )
    carried = initial
    first_row = jnp.int32(0)
    key_piece = lax.all_gather(k_proj, "seq", axis=0, tiled=True)
    value_piece = lax.all_gather(hyena_out, "seq", axis=0, tiled=True)
    piece_rows = key_piece.shape[0]
    block_rows = math.gcd(piece_rows, 512)
    block_count = piece_rows // block_rows
    key_blocks = key_piece.reshape(block_count, block_rows, head_count, HEAD_SIZE)
    value_blocks = value_piece.reshape(block_count, block_rows, head_count, HEAD_SIZE)

    def visit(running, block_item):
        key_blk, value_blk, block_number = block_item
        key_start = first_row + block_number * block_rows

        def attend(current):
            weighted, run_max, total_sum = current
            scores = (
                jnp.einsum("qhd,khd->hqk", queries, key_blk, preferred_element_type=jnp.float32)
                * score_scale
            )
            key_pos = key_start + jnp.arange(block_rows, dtype=jnp.int32)
            allowed = key_pos[None, None, :] <= query_pos[None, :, None]
            masked = jnp.where(allowed, scores, -jnp.inf)
            new_max = jnp.maximum(run_max, jnp.max(masked, axis=-1))
            weights = jnp.exp(masked - new_max[..., None])
            factor = jnp.exp(run_max - new_max)
            new_total = total_sum * factor + jnp.sum(weights, axis=-1)
            new_weighted = weighted * factor[..., None] + jnp.einsum(
                "hqk,khd->hqd",
                weights.astype(jnp.bfloat16),
                value_blk,
                preferred_element_type=jnp.float32,
            )
            return (new_weighted, new_max, new_total)

        def keep_state(current):
            return current

        return (lax.cond(key_start <= last_query, attend, keep_state, running), None)

    carried, unused = lax.scan(
        visit, carried, (key_blocks, value_blocks, jnp.arange(block_count, dtype=jnp.int32))
    )
    weighted, run_max, total_sum = carried
    attended = (
        (weighted / total_sum[..., None])
        .transpose(1, 0, 2)
        .reshape(tok_rows, chan_width)
        .astype(jnp.bfloat16)
    )
    summed = lax.psum_scatter(
        lax.dot_general(
            out_weight, attended, (((0,), (1,)), ((), ())), preferred_element_type=jnp.float32
        ).astype(jnp.bfloat16),
        "head",
        scatter_dimension=0,
        tiled=True,
    ).astype(jnp.float32)
    return (hyena_out, summed.T.astype(jnp.bfloat16))


def solution(mesh):
    return jax.shard_map(
        per_device,
        mesh=mesh,
        in_specs=(
            P(("batch", "seq"), None, "head"),
            P(None, None, "head"),
            P(None, "head"),
            P(("batch", "seq"), "head"),
            P(("batch", "seq"), "head"),
            P("head", None),
        ),
        out_specs=(P(("batch", "seq"), "head"), P(("batch", "seq"), "head")),
        check_vma=False,
    )
```

profile of v0, /device:TPU:0, one launch (start us, length us, event | category | flops | bytes accessed | tf_op | source)
XLA Modules:
  0.0 636.0 jit_solution(6922452532543686896)
XLA Ops:
  10.6 16.9 %rev.6 = f32[3,6144]{1,0:T(4,128)S(1)} reverse(f32[3,6144]{1,0:T(4,128)} %bitcast.76), dimensions={0} | reverse | bytes 147456 | tf_op jit(solution)/shard_map/rev | solution.py:19
  27.6 7.8 %pad_maximum_fusion = bf16[514,3,2048]{2,0,1:T(8,128)(2,1)} fusion(bf16[512,3,2048]{2,0,1:T(8,128)(2,1)} %param.10, bf16[2,3,2048]{2,0,1:T(2,128)(2,1)S(1)} %collective-permute-done), kind=kLoop, calls=%fused_computation.37 | loop fusion | flops 12632064 | bytes 12632064 | tf_op jit(solution)/shard_map/concatenate | solution.py:40
  35.4 9.7 %copy.12 = bf16[514,3,2048]{0,2,1:T(8,128)(2,1)} copy(bf16[514,3,2048]{2,0,1:T(8,128)(2,1)} %pad_maximum_fusion) | data formatting | bytes 12632064 | tf_op jit(solution)/shard_map/concatenate | solution.py:40
  45.1 7.0 %pad = bf16[1,520,6144]{1,2,0:T(8,128)(2,1)} pad(bf16[1,514,6144]{1,2,0:T(8,128)(2,1)} %bitcast.69, bf16[]{:T(256)} %constant.51), padding=0_0x0_6x0_0 | pad | bytes 12705794 | tf_op jit(solution)/shard_map/broadcast_in_dim;reshape | solution.py:21
  52.1 20.5 %reshape.76 = bf16[1,8,65,6144]{2,1,3,0:T(8,128)(2,1)} reshape(bf16[1,520,6144]{1,2,0:T(8,128)(2,1)} %pad) | data formatting | bytes 12779520 | tf_op jit(solution)/shard_map/conv_general_dilated | solution.py:20
  72.7 16.8 %copy.15 = bf16[1,8,65,6144]{3,1,2,0:T(8,128)(2,1)} copy(bf16[1,8,65,6144]{2,1,3,0:T(8,128)(2,1)} %reshape.76) | data formatting | bytes 12779520 | tf_op jit(solution)/shard_map/conv_general_dilated | solution.py:20
  90.4 11.8 %fusion.30 = f32[8,65,6144]{2,0,1:T(8,128)} fusion(f32[3,1,6144]{2,1,0:T(1,128)S(1)} %broadcast_in_dim.40, bf16[1,7,2,6144]{3,1,2,0:T(8,128)(2,1)S(1)} %slice.26, bf16[1,8,65,6144]{3,1,2,0:T(8,128)(2,1)} %copy.15, pred[8,65]{0,1:T(8,128)(4,1)S(1)} %copy-done.4), kind=kOutput, calls=%fused_computation.33 | convolution fusion | flops 137969664 | bytes 19415560 | tf_op jit(solution)/shard_map/conv_general_dilated | solution.py:20
  102.2 17.2 %copy.16 = f32[8,65,6144]{2,1,0:T(8,128)} copy(f32[8,65,6144]{2,0,1:T(8,128)} %fusion.30) | data formatting | bytes 25559040 | tf_op jit(solution)/shard_map/conv_general_dilated | solution.py:20
  119.4 11.3 %reshape.72 = f32[1,520,6144]{2,1,0:T(8,128)} reshape(f32[8,65,6144]{2,1,0:T(8,128)} %copy.16) | data formatting | bytes 25559040 | tf_op jit(solution)/shard_map/conv_general_dilated | solution.py:20
  130.7 10.6 %slice.27 = f32[1,512,6144]{2,1,0:T(8,128)} slice(f32[1,520,6144]{2,1,0:T(8,128)} %reshape.72), slice={[0:1], [0:512], [0:6144]} | slice | bytes 25165824 | tf_op jit(solution)/shard_map/conv_general_dilated | solution.py:20
  141.3 12.8 %copy.17 = f32[1,512,6144]{1,2,0:T(8,128)} copy(f32[1,512,6144]{2,1,0:T(8,128)} %slice.27) | data formatting | bytes 25165824 | tf_op jit(solution)/shard_map/conv_general_dilated | solution.py:20
  154.0 7.7 %fusion.44 = (f32[512,1,2048]{0,2,1:T(8,128)}, bf16[512,1,2048]{0,2,1:T(8,128)(2,1)S(1)}) fusion(f32[512,3,2048]{0,2,1:T(8,128)} %bitcast.66), kind=kLoop, calls=%fused_computation.51 | loop fusion | flops 2097152 | bytes 18874368 | tf_op jit(solution)/shard_map/slice | solution.py:49
  162.8 5.4 collective-permute-start.1
  168.2 5.2 rev.7
  173.3 5.5 copy.33
  178.8 4.0 maximum_bitcast_fusion
  182.8 11.5 %copy.20 = bf16[1,639,2048]{2,0,1:T(2,128)(2,1)} copy(bf16[1,639,2048]{1,2,0:T(8,128)(2,1)} %maximum_bitcast_fusion) | data formatting | bytes 5234688 | tf_op jit(solution)/shard_map/broadcast_in_dim | solution.py:21
  194.4 48.5 %fusion.39 = f32[1,512,2048]{2,0,1:T(1,128)S(1)} fusion(bf16[1,639,2048]{2,0,1:T(2,128)(2,1)} %copy.20, f32[128,1,2048]{2,0,1:T(8,128)S(1)} %bitcast.75), kind=kOutput, calls=%fused_computation.45 | convolution fusion | flops 1610612736 | bytes 7860224 | tf_op jit(solution)/shard_map/conv_general_dilated | solution.py:20
  248.4 3.0 copy.24
  251.5 10.9 %copy.34 = bf16[256,8,16,128]{3,2,1,0:T(8,128)(2,1)} copy(bf16[256,8,16,128]{3,1,2,0:T(8,128)(2,1)} %bitcast.71) | data formatting | bytes 16777216
  262.3 8.8 %copy.23 = bf16[4,512,16,128]{3,1,2,0:T(8,128)(2,1)} copy(bf16[4,512,16,128]{3,2,1,0:T(8,128)(2,1)} %bitcast.67) | data formatting | bytes 16777216
  271.2 33.2 %all-gather.5.cloned.1.call-done = bf16[2048,2048]{1,0:T(8,128)(2,1)} async-done(((bf16[512,2048]{1,0:T(8,128)(2,1)}), bf16[2048,2048]{1,0:T(8,128)(2,1)}) %all-gather.5.cloned.1.call-update) | async-done | bytes 8388624 | tf_op jit(solution)/shard_map/all_gather | solution.py:64
  304.4 9.8 %copy.35 = bf16[256,8,16,128]{3,2,1,0:T(8,128)(2,1)} copy(bf16[256,8,16,128]{3,1,2,0:T(8,128)(2,1)} %bitcast.72) | data formatting | bytes 16777216
  314.1 8.8 %copy.25 = bf16[4,512,16,128]{3,1,2,0:T(8,128)(2,1)} copy(bf16[4,512,16,128]{3,2,1,0:T(8,128)(2,1)} %bitcast.68) | data formatting | bytes 16777216
  325.4 35.2 %while.15 = (s32[]{:T(128)}, f32[16,512,128]{2,1,0:T(8,128)}, f32[16,512]{1,0:T(8,128)S(1)}, f32[16,512]{1,0:T(8,128)S(1)}, s32[4]{0:T(128)S(1)}, /*index=5*/s32...) while((s32[]{:T(128)}, f32[16,512,128]{2,1,0:T(8,128)}, ...), condition=%wide.region_5.6_spmd.clone, body=%wide.region_0.5_spmd.clone.sunk | while | flops 2195997696 | bytes 66598184 | solution.py:101
  326.9 30.0 %conditional.3 = ((f32[16,512,128]{2,1,0:T(8,128)}, f32[16,512]{1,0:T(8,128)S(1)}, f32[16,512]{1,0:T(8,128)S(1)})) conditional(s32[]{:T(128)} %convert_element_type.60, (f32[16,512,128]{2,1,0:T(8,128)}, f32[16,512]{1,0:T(8,128)S(1)}, f32[16,512]{1,0:T(8,128)S(1)}) %tuple.46, (s32[]{:T(128)}, s32[]{:T(128)}, bf16[4,512,16,128]{3,1,2,0:T(8,128)(2,1)}, ...), branch_computations={%region_1.1_spmd, %region_2.4_spmd} | conditional | flops 2195997696 | bytes 66595880 | solution.py:99
  327.1 8.8 %fusion.4 = (f32[16,512]{1,0:T(8,128)S(1)}, f32[16,512,512]{2,1,0:T(8,128)}) fusion(pred[512,512]{0,1:T(8,128)(4,1)S(1)} %broadcast_compare_fusion, bf16[512,16,128]{2,0,1:T(8,128)(2,1)S(1)} %get-tuple-element.117, bf16[4,512,16,128]{3,1,2,0:T(8,128)(2,1)} %get-tuple-element.115, s32[]{:T(128)} %get-tuple-element.116), kind=kOutput, calls=%fused_computation.5 | convolution fusion | flops 1086316544 | bytes 21266944 | tf_op jit(solution)/shard_map/while/body/eval_jaxpr/cond/branch_1_fun/qhd,khd->hqk/dot_general | solution.py:78
  335.9 9.1 %fusion.2 = f32[16,512]{1,0:T(8,128)S(1)} fusion(f32[16,512,512]{2,1,0:T(8,128)} %get-tuple-element.212, f32[16,512]{1,0:T(8,128)S(1)} %max.4, pred[512,512]{0,1:T(8,128)(4,1)S(1)} %broadcast_compare_fusion), kind=kLoop, calls=%fused_computation.3 | loop fusion | flops 16769024 | bytes 17104896 | tf_op jit(solution)/shard_map/while/body/eval_jaxpr/cond/branch_1_fun/reduce_sum | solution.py:87
  345.1 11.7 %multiply_add_fusion = f32[16,512,128]{2,1,0:T(8,128)} fusion(f32[16,512,128]{2,1,0:T(8,128)} %get-tuple-element.111, f32[16,512]{1,0:T(8,128)S(1)} %get-tuple-element.210, bf16[4,512,16,128]{3,1,2,0:T(8,128)(2,1)} %get-tuple-element.118, s32[]{:T(128)} %get-tuple-element.116, f32[16,512,512]{2,1,0:T(8,128)} %get-tuple-element.212, f32[16,512]{1,0:T(8,128)S(1)} %max.4, ...), kind=kOutput, calls=%fused_computation.11 | convolution fusion | flops 1092616192 | bytes 27591168 | tf_op jit(solution)/shard_map/while/body/eval_jaxpr/cond/branch_1_fun/hqk,khd->hqd/dot_general | solution.py:88
  360.6 5.4 copy.26
  368.8 26.1 %fusion.25 = bf16[8192,512]{0,1:T(8,128)(2,1)} fusion(bf16[512,2048]{0,1:T(8,128)(2,1)S(1)} %bitcast.74, bf16[2048,8192]{1,0:T(8,128)(2,1)} %param.15), kind=kOutput, calls=%fused_computation.29 | convolution fusion | flops 17184063488 | bytes 44040192 | tf_op jit(solution)/shard_map/dot_general | solution.py:112
  395.0 234.0 %reduce-scatter.2.cloned.1.call-done = bf16[2048,512]{0,1:T(8,128)(2,1)} async-done(((bf16[8192,512]{0,1:T(8,128)(2,1)}), bf16[2048,512]{0,1:T(8,128)(2,1)}) %reduce-scatter.2.cloned.1.call-update) | async-done | bytes 2097168 | tf_op jit(solution)/shard_map/reduce_scatter | solution.py:111
  (47 shorter events, 18.9 us)
Async XLA Ops:
  7.2 244.3 %all-gather.3.cloned.1.call-start = ((), (), s32[]{:S(2)}) async-start(), calls=%async_computation.1 | async-start | bytes 10485760 | tf_op jit(solution)/shard_map/all_gather | solution.py:63
  8.1 19.4 %collective-permute-start = (bf16[2,3,2048]{2,0,1:T(2,128)(2,1)S(1)}, bf16[2,3,2048]{2,0,1:T(2,128)(2,1)S(1)}, u32[]{:S(2)}, u32[]{:S(2)}) collective-permute-start(bf16[2,3,2048]{2,0,1:T(2,128)(2,1)S(1)} %slice.18), channel_id=1, source_target_pairs={{0,8},{8,16},{16,24},{1,9},{9,17},{17,25},{2,10},{10,18},{18,26},{... | collective-permute-start | bytes 73736 | tf_op jit(solution)/shard_map/ppermute | solution.py:13
  10.5 293.8 %all-gather.5.cloned.1.call-start = ((), (), s32[]{:S(2)}) async-start(), calls=%async_computation.2 | async-start | bytes 10485760 | tf_op jit(solution)/shard_map/all_gather | solution.py:64
  72.7 17.8 %copy-start.4 = (pred[8,65]{0,1:T(8,128)(4,1)S(1)}, pred[8,65]{0,1:T(8,128)(4,1)}, u32[]{:S(2)}) copy-start(pred[8,65]{0,1:T(8,128)(4,1)} %constant.55) | copy-start | bytes 1564
  154.0 14.1 %copy-start.2 = (f32[128,2048]{1,0:T(8,128)S(1)}, f32[128,2048]{1,0:T(8,128)}, u32[]{:S(2)}) copy-start(f32[128,2048]{1,0:T(8,128)} %param.12) | copy-start | bytes 3145732
  162.8 16.0 %collective-permute-start.1 = (bf16[127,2048]{0,1:T(8,128)(2,1)}, bf16[127,2048]{0,1:T(8,128)(2,1)}, u32[]{:S(2)}, u32[]{:S(2)}) collective-permute-start(bf16[127,2048]{0,1:T(8,128)(2,1)} %slice_bitcast_fusion), channel_id=1, source_target_pairs={{0,8},{8,16},{16,24},{1,9},{9,17},{17,25},{2,10},{10,18},{18,26},{... | collective-permute-start | bytes 1560584 | tf_op jit(solution)/shard_map/ppermute | solution.py:13
  178.8 15.6 %copy-start.3 = (f32[128,2048]{1,0:T(8,128)S(1)}, f32[128,2048]{1,0:T(8,128)}, u32[]{:S(2)}) copy-start(f32[128,2048]{1,0:T(8,128)} %rev.7) | copy-start | bytes 3145732
  194.4 48.5 %copy-start = (f32[512,1,2048]{2,0,1:T(8,128)S(1)}, f32[512,1,2048]{2,0,1:T(8,128)}, u32[]{:S(2)}) copy-start(f32[512,1,2048]{2,0,1:T(8,128)} %copy.33) | copy-start | bytes 12582916
  242.9 2.8 copy-start.1
  245.6 383.4 %reduce-scatter.2.cloned.1.call-start = ((), (), s32[]{:S(2)}) async-start(), calls=%async_computation.3 | async-start | bytes 10485760 | tf_op jit(solution)/shard_map/reduce_scatter | solution.py:111
Sparse Core Ops, SparseCore 0:
  10.6 60.8 all-gather.2
  245.7 58.5 all-gather.4
  395.1 233.8 reduce-scatter.1
where the time goes:
time: 644 us; the launch traced here: 636 us
  waiting for transfers between devices  267 us (41%)
  local copies, waits for them, and re-layouts  202 us (31%)
  matrix products  107 us (17%)
  other arithmetic  34.5 us (5%)
  between operations  14.4 us (2%)
  starting transfers between devices  7.87 us (1%)
    reduce_scatter x1, waiting for transfers between devices, per_device(): lax.psum_scatter(lax.dot_general(out_weight, attended, (((0,), (1,)), (()...  234 us
    conv_general_dilated x7, local copies, waits for them, and re-layouts, causal_depthwise(): lax.conv_general_dilated(window[None], kernel, (1,), 'VALID', feature_gro...  90.1 us
    conv_general_dilated x2, matrix products, causal_depthwise(): lax.conv_general_dilated(window[None], kernel, (1,), 'VALID', feature_gro...  60.3 us
    unnamed x17, local copies, waits for them, and re-layouts  49.5 us
    all_gather x1, waiting for transfers between devices, per_device(): value_piece = lax.all_gather(hyena_out, 'seq', axis=0, tiled=True)  33.2 us
    dot_general x1, matrix products, per_device(): lax.dot_general(out_weight, attended, (((0,), (1,)), ((), ())), preferred...  26.1 us
    rev x2, local copies, waits for them, and re-layouts, causal_depthwise(): kernel = taps[::-1][:, None, :]  22.1 us
  transfers between devices with their start and end apart: 5, of which 2 were waited for; matrix products, arithmetic and copies ran while one was open for 40% of the time, Pallas kernels for 0%

commit v1 on v0

--- a/solution.py
+++ b/solution.py
@@ -5,6 +5,28 @@
 from jax.sharding import PartitionSpec as P
 
 HEAD_SIZE = 128
+
+
+def in_order(tiles, dim):
+    tiles = jnp.moveaxis(tiles, 0, dim)
+    dims = tiles.shape
+    return tiles.reshape(*dims[:dim], dims[dim] * dims[dim + 1], *dims[dim + 2 :])
+
+
+def gather_around(array, axis, dim):
+    size = lax.axis_size(axis)
+    pairs = [(i, (i + 1) % size) for i in range(size)]
+    back = [(b, a) for a, b in pairs]
+    lower, upper = ([], [])
+    for step in range(size - 1):
+        if step % 2 == 0:
+            lower.append(lax.ppermute(lower[-1] if lower else array, axis, pairs))
+        else:
+            upper.append(lax.ppermute(upper[-1] if upper else array, axis, back))
+    pieces = jnp.stack([*lower[::-1], array, *upper])
+    shift = lax.axis_index(axis) - len(lower)
+    pieces = pieces[(jnp.arange(size) - shift) % size]
+    return in_order(pieces, dim)
 
 
 def passed_along(x, axis, by):
@@ -61,7 +83,7 @@
     carried = initial
     first_row = jnp.int32(0)
     key_piece = lax.all_gather(k_proj, "seq", axis=0, tiled=True)
-    value_piece = lax.all_gather(hyena_out, "seq", axis=0, tiled=True)
+    value_piece = gather_around(hyena_out, "seq", 0)
     piece_rows = key_piece.shape[0]
     block_rows = math.gcd(piece_rows, 512)
     block_count = piece_rows // block_rows

time: 644 us -> 729 us (1.13)
  local copies, waits for them, and re-layouts: 202 us -> 233 us
  other arithmetic: 34.5 us -> 63.5 us
  waiting for transfers between devices: 267 us -> 287 us
    ppermute x0 -> x3, waiting for transfers between devices: none -> 54.3 us  [the longest x2 54.3 us: gather_around(): lower.append(lax.ppermute(lower[-1] if lower else array, axis, pairs))]
    all_gather x1 -> x0, waiting for transfers between devices: 33.2 us -> none  [per_device(): value_piece = lax.all_gather(hyena_out, 'seq', axis=0, tiled=True)]
    another operation x0 -> x1, other arithmetic: none -> 21.2 us  [gather_around(): pieces = jnp.stack([*lower[::-1], array, *upper])]
    gather x0 -> x5, local copies, waits for them, and re-layouts: none -> 20.7 us  [gather_around(): pieces = pieces[(jnp.arange(size) - shift) % size]]
    another operation x0 -> x3, local copies, waits for them, and re-layouts: none -> 18.4 us  [gather_around(): pieces = jnp.stack([*lower[::-1], array, *upper])]
    unnamed x17 -> x16, local copies, waits for them, and re-layouts: 49.5 us -> 41 us
    unnamed x0 -> x1, other arithmetic: none -> 7.76 us
  transfers between devices with their start and end apart: 5 -> 7, of which waited for: 2 -> 3; matrix products, arithmetic and copies ran while one was open for 40% -> 25% of each run, Pallas kernels for 0% -> 0%
where the time goes in v1:
time: 729 us; the launch traced here: 721 us
  waiting for transfers between devices  287 us (39%)
  local copies, waits for them, and re-layouts  233 us (32%)
  matrix products  110 us (15%)
  other arithmetic  63.5 us (9%)
  between operations  14.4 us (2%)
  starting transfers between devices  9.53 us (1%)
    reduce_scatter x1, waiting for transfers between devices, per_device(): lax.psum_scatter(lax.dot_general(out_weight, attended, (((0,), (1,)), (()...  233 us
    conv_general_dilated x7, local copies, waits for them, and re-layouts, causal_depthwise(): lax.conv_general_dilated(window[None], kernel, (1,), 'VALID', feature_gro...  90.5 us
    conv_general_dilated x2, matrix products, causal_depthwise(): lax.conv_general_dilated(window[None], kernel, (1,), 'VALID', feature_gro...  63.3 us
    ppermute x2, waiting for transfers between devices, gather_around(): lower.append(lax.ppermute(lower[-1] if lower else array, axis, pairs))  54.3 us
    unnamed x16, local copies, waits for them, and re-layouts  41 us
    dot_general x1, matrix products, per_device(): lax.dot_general(out_weight, attended, (((0,), (1,)), ((), ())), preferred...  25.9 us
    rev x2, local copies, waits for them, and re-layouts, causal_depthwise(): kernel = taps[::-1][:, None, :]  22 us
    another operation x1, other arithmetic, gather_around(): pieces = jnp.stack([*lower[::-1], array, *upper])  21.2 us
  transfers between devices with their start and end apart: 7, of which 3 were waited for; matrix products, arithmetic and copies ran while one was open for 25% of the time, Pallas kernels for 0%

profile of v1, /device:TPU:0, one launch (start us, length us, event | category | flops | bytes accessed | tf_op | source)
XLA Modules:
  0.0 721.0 jit_solution(6162801459740739673)
XLA Ops:
  10.5 16.9 %rev.6 = f32[3,6144]{1,0:T(4,128)S(1)} reverse(f32[3,6144]{1,0:T(4,128)} %bitcast.85), dimensions={0} | reverse | bytes 147456 | tf_op jit(solution)/shard_map/rev | solution.py:41
  27.4 7.8 %pad_maximum_fusion.1 = bf16[514,3,2048]{2,0,1:T(8,128)(2,1)} fusion(bf16[512,3,2048]{2,0,1:T(8,128)(2,1)} %param.10, bf16[2,3,2048]{2,0,1:T(2,128)(2,1)S(1)} %collective-permute-done), kind=kLoop, calls=%fused_computation.42 | loop fusion | flops 12632064 | bytes 12632064 | tf_op jit(solution)/shard_map/concatenate | solution.py:62
  35.3 9.7 %copy.74 = bf16[514,3,2048]{0,2,1:T(8,128)(2,1)} copy(bf16[514,3,2048]{2,0,1:T(8,128)(2,1)} %pad_maximum_fusion.1) | data formatting | bytes 12632064 | tf_op jit(solution)/shard_map/concatenate | solution.py:62
  45.0 7.0 pad
  52.0 20.5 %reshape.138 = bf16[1,8,65,6144]{2,1,3,0:T(8,128)(2,1)} reshape(bf16[1,520,6144]{1,2,0:T(8,128)(2,1)} %pad) | data formatting | bytes 12779520 | tf_op jit(solution)/shard_map/conv_general_dilated | solution.py:42
  72.5 16.9 %copy.77 = bf16[1,8,65,6144]{3,1,2,0:T(8,128)(2,1)} copy(bf16[1,8,65,6144]{2,1,3,0:T(8,128)(2,1)} %reshape.138) | data formatting | bytes 12779520 | tf_op jit(solution)/shard_map/conv_general_dilated | solution.py:42
  90.3 11.6 %fusion.30 = f32[8,65,6144]{2,0,1:T(8,128)} fusion(f32[3,1,6144]{2,1,0:T(1,128)S(1)} %broadcast_in_dim.41, bf16[1,7,2,6144]{3,1,2,0:T(8,128)(2,1)S(1)} %slice.30, bf16[1,8,65,6144]{3,1,2,0:T(8,128)(2,1)} %copy.77, pred[8,65]{0,1:T(8,128)(4,1)S(1)} %copy-done.4), kind=kOutput, calls=%fused_computation.38 | convolution fusion | flops 137969664 | bytes 19415560 | tf_op jit(solution)/shard_map/conv_general_dilated | solution.py:42
  101.9 17.2 %copy.78 = f32[8,65,6144]{2,1,0:T(8,128)} copy(f32[8,65,6144]{2,0,1:T(8,128)} %fusion.30) | data formatting | bytes 25559040 | tf_op jit(solution)/shard_map/conv_general_dilated | solution.py:42
  119.1 11.3 %reshape.118 = f32[1,520,6144]{2,1,0:T(8,128)} reshape(f32[8,65,6144]{2,1,0:T(8,128)} %copy.78) | data formatting | bytes 25559040 | tf_op jit(solution)/shard_map/conv_general_dilated | solution.py:42
  130.4 10.6 %slice.31 = f32[1,512,6144]{2,1,0:T(8,128)} slice(f32[1,520,6144]{2,1,0:T(8,128)} %reshape.118), slice={[0:1], [0:512], [0:6144]} | slice | bytes 25165824 | tf_op jit(solution)/shard_map/conv_general_dilated | solution.py:42
  140.9 13.1 %copy.79 = f32[1,512,6144]{1,2,0:T(8,128)} copy(f32[1,512,6144]{2,1,0:T(8,128)} %slice.31) | data formatting | bytes 25165824 | tf_op jit(solution)/shard_map/conv_general_dilated | solution.py:42
  154.1 7.7 %fusion.47 = (f32[512,1,2048]{0,2,1:T(8,128)}, bf16[512,1,2048]{0,2,1:T(8,128)(2,1)S(1)}) fusion(f32[512,3,2048]{0,2,1:T(8,128)} %bitcast.77), kind=kLoop, calls=%fused_computation.65 | loop fusion | flops 2097152 | bytes 18874368 | tf_op jit(solution)/shard_map/slice | solution.py:71
  173.4 11.3 %copy.101 = f32[512,1,2048]{2,1,0:T(1,128)} copy(f32[512,1,2048]{0,2,1:T(8,128)} %get-tuple-element.245) | data formatting | bytes 8388608
  184.7 5.5 copy.99
  194.3 11.5 %copy.82 = bf16[1,639,2048]{2,0,1:T(2,128)(2,1)} copy(bf16[1,639,2048]{1,2,0:T(8,128)(2,1)} %maximum_bitcast_fusion.1) | data formatting | bytes 5234688 | tf_op jit(solution)/shard_map/broadcast_in_dim | solution.py:43
  205.8 51.7 %fusion.38 = (bf16[1,512,2048]{2,0,1:T(2,128)(2,1)}, f32[1,512,2048]{2,0,1:T(1,128)S(1)}) fusion(f32[512,1,2048]{2,1,0:T(1,128)} %copy.101, bf16[1,639,2048]{2,0,1:T(2,128)(2,1)} %copy.82, f32[128,1,2048]{2,0,1:T(8,128)S(1)} %bitcast.84), kind=kOutput, calls=%fused_computation.48 | convolution fusion | flops 1612709888 | bytes 14151680 | tf_op jit(solution)/shard_map/conv_general_dilated | solution.py:42
  262.0 45.9 %collective-permute-done.2 = bf16[512,2048]{1,0:T(8,128)(2,1)} collective-permute-done((bf16[512,2048]{1,0:T(8,128)(2,1)}, bf16[512,2048]{1,0:T(8,128)(2,1)}, u32[]{:S(2)}, u32[]{:S(2)}) %collective-permute-start.2) | collective-permute-done | bytes 2097184 | tf_op jit(solution)/shard_map/ppermute | solution.py:23
  318.5 6.8 copy.87
  325.3 8.4 %collective-permute-done.3 = bf16[512,2048]{1,0:T(8,128)(2,1)} collective-permute-done((bf16[512,2048]{1,0:T(8,128)(2,1)}, bf16[512,2048]{1,0:T(8,128)(2,1)}, u32[]{:S(2)}, u32[]{:S(2)}) %collective-permute-start.3) | collective-permute-done | bytes 2097184 | tf_op jit(solution)/shard_map/ppermute | solution.py:23
  333.7 6.8 copy.85
  340.5 21.2 %pad_maximum_fusion = bf16[4,512,2048]{2,0,1:T(4,128)(2,1)S(1)} fusion(bf16[1,512,2048]{2,0,1:T(2,128)(2,1)} %copy.87, bf16[1,512,2048]{2,0,1:T(2,128)(2,1)} %get-tuple-element.249, bf16[1,512,2048]{2,0,1:T(2,128)(2,1)S(1)} %copy.86, bf16[1,512,2048]{2,0,1:T(2,128)(2,1)} %copy.85), kind=kLoop, calls=%fused_computation.33 | loop fusion | flops 33554432 | bytes 16777216 | tf_op jit(solution)/shard_map/stack | solution.py:26
  382.4 7.8 %copy_bitcast_fusion = bf16[4,512,16,128]{3,1,2,0:T(8,128)(2,1)} fusion(bf16[4,512,1024]{2,1,0:T(8,128)(2,1)} %gather_fusion.1, bf16[4,512,1024]{2,1,0:T(8,128)(2,1)} %gather_fusion), kind=kLoop, calls=%fused_computation.32 | loop fusion | flops 16777216 | bytes 16777216
  390.2 9.8 %copy.104 = bf16[256,8,16,128]{3,2,1,0:T(8,128)(2,1)} copy(bf16[256,8,16,128]{3,1,2,0:T(8,128)(2,1)} %bitcast.81) | data formatting | bytes 16777216
  400.0 8.8 %copy.90 = bf16[4,512,16,128]{3,1,2,0:T(8,128)(2,1)} copy(bf16[4,512,16,128]{3,2,1,0:T(8,128)(2,1)} %bitcast.78) | data formatting | bytes 16777216
  411.3 35.5 %while.15 = (s32[]{:T(128)}, f32[16,512,128]{2,1,0:T(8,128)}, f32[16,512]{1,0:T(8,128)S(1)}, f32[16,512]{1,0:T(8,128)S(1)}, s32[4]{0:T(128)S(1)}, /*index=5*/s32...) while((s32[]{:T(128)}, f32[16,512,128]{2,1,0:T(8,128)}, ...), condition=%wide.region_5.6_spmd.clone, body=%wide.region_0.5_spmd.clone.sunk | while | flops 2195997696 | bytes 66598184 | solution.py:123
  413.0 29.8 %conditional.3 = ((f32[16,512,128]{2,1,0:T(8,128)}, f32[16,512]{1,0:T(8,128)S(1)}, f32[16,512]{1,0:T(8,128)S(1)})) conditional(s32[]{:T(128)} %convert_element_type.65, (f32[16,512,128]{2,1,0:T(8,128)}, f32[16,512]{1,0:T(8,128)S(1)}, f32[16,512]{1,0:T(8,128)S(1)}) %tuple.51, (s32[]{:T(128)}, s32[]{:T(128)}, bf16[4,512,16,128]{3,1,2,0:T(8,128)(2,1)}, ...), branch_computations={%region_1.1_spmd, %region_2.4_spmd} | conditional | flops 2195997696 | bytes 66595880 | solution.py:121
  413.2 8.8 %fusion.4 = (f32[16,512]{1,0:T(8,128)S(1)}, f32[16,512,512]{2,1,0:T(8,128)}) fusion(pred[512,512]{0,1:T(8,128)(4,1)S(1)} %broadcast_compare_fusion, bf16[512,16,128]{2,0,1:T(8,128)(2,1)S(1)} %get-tuple-element.117, bf16[4,512,16,128]{3,1,2,0:T(8,128)(2,1)} %get-tuple-element.115, s32[]{:T(128)} %get-tuple-element.116), kind=kOutput, calls=%fused_computation.7 | convolution fusion | flops 1086316544 | bytes 21266944 | tf_op jit(solution)/shard_map/while/body/eval_jaxpr/cond/branch_1_fun/qhd,khd->hqk/dot_general | solution.py:100
  422.0 9.1 %fusion.2 = f32[16,512]{1,0:T(8,128)S(1)} fusion(f32[16,512,512]{2,1,0:T(8,128)} %get-tuple-element.242, f32[16,512]{1,0:T(8,128)S(1)} %max.4, pred[512,512]{0,1:T(8,128)(4,1)S(1)} %broadcast_compare_fusion), kind=kLoop, calls=%fused_computation.5 | loop fusion | flops 16769024 | bytes 17104896 | tf_op jit(solution)/shard_map/while/body/eval_jaxpr/cond/branch_1_fun/reduce_sum | solution.py:109
  431.2 11.6 %multiply_add_fusion = f32[16,512,128]{2,1,0:T(8,128)} fusion(f32[16,512,128]{2,1,0:T(8,128)} %get-tuple-element.111, f32[16,512]{1,0:T(8,128)S(1)} %get-tuple-element.240, bf16[4,512,16,128]{3,1,2,0:T(8,128)(2,1)} %get-tuple-element.118, s32[]{:T(128)} %get-tuple-element.116, f32[16,512,512]{2,1,0:T(8,128)} %get-tuple-element.242, f32[16,512]{1,0:T(8,128)S(1)} %max.4, ...), kind=kOutput, calls=%fused_computation.13 | convolution fusion | flops 1092616192 | bytes 27591168 | tf_op jit(solution)/shard_map/while/body/eval_jaxpr/cond/branch_1_fun/hqk,khd->hqd/dot_general | solution.py:110
  446.7 5.4 copy.93
  454.9 25.9 %fusion.25 = bf16[8192,512]{0,1:T(8,128)(2,1)} fusion(bf16[512,2048]{0,1:T(8,128)(2,1)S(1)} %bitcast.83, bf16[2048,8192]{1,0:T(8,128)(2,1)} %param.15), kind=kOutput, calls=%fused_computation.31 | convolution fusion | flops 17184063488 | bytes 44040192 | tf_op jit(solution)/shard_map/dot_general | solution.py:134
  480.9 233.1 %reduce-scatter.2.cloned.1.call-done = bf16[2048,512]{0,1:T(8,128)(2,1)} async-done(((bf16[8192,512]{0,1:T(8,128)(2,1)}), bf16[2048,512]{0,1:T(8,128)(2,1)}) %reduce-scatter.2.cloned.1.call-update) | async-done | bytes 2097168 | tf_op jit(solution)/shard_map/reduce_scatter | solution.py:133
  (61 shorter events, 63.9 us)
Async XLA Ops:
  7.2 383.0 %all-gather.2.cloned.1.call-start = ((), (), s32[]{:S(2)}) async-start(), calls=%async_computation.1 | async-start | bytes 10485760 | tf_op jit(solution)/shard_map/all_gather | solution.py:85
  8.1 19.3 %collective-permute-start = (bf16[2,3,2048]{2,0,1:T(2,128)(2,1)S(1)}, bf16[2,3,2048]{2,0,1:T(2,128)(2,1)S(1)}, u32[]{:S(2)}, u32[]{:S(2)}) collective-permute-start(bf16[2,3,2048]{2,0,1:T(2,128)(2,1)S(1)} %slice.18), channel_id=1, source_target_pairs={{0,8},{8,16},{16,24},{1,9},{9,17},{17,25},{2,10},{10,18},{18,26},{... | collective-permute-start | bytes 73736 | tf_op jit(solution)/shard_map/ppermute | solution.py:35
  72.5 17.8 %copy-start.4 = (pred[8,65]{0,1:T(8,128)(4,1)S(1)}, pred[8,65]{0,1:T(8,128)(4,1)}, u32[]{:S(2)}) copy-start(pred[8,65]{0,1:T(8,128)(4,1)} %constant.74) | copy-start | bytes 1564
  154.1 14.2 %copy-start.2 = (f32[128,2048]{1,0:T(8,128)S(1)}, f32[128,2048]{1,0:T(8,128)}, u32[]{:S(2)}) copy-start(f32[128,2048]{1,0:T(8,128)} %param.12) | copy-start | bytes 3145732
  162.8 27.4 %collective-permute-start.1 = (bf16[127,2048]{0,1:T(8,128)(2,1)}, bf16[127,2048]{0,1:T(8,128)(2,1)}, u32[]{:S(2)}, u32[]{:S(2)}) collective-permute-start(bf16[127,2048]{0,1:T(8,128)(2,1)} %slice_bitcast_fusion), channel_id=1, source_target_pairs={{0,8},{8,16},{16,24},{1,9},{9,17},{17,25},{2,10},{10,18},{18,26},{... | collective-permute-start | bytes 1560584 | tf_op jit(solution)/shard_map/ppermute | solution.py:35
  168.2 545.8 %reduce-scatter.2.cloned.1.call-start = ((), (), s32[]{:S(2)}) async-start(), calls=%async_computation.2 | async-start | bytes 10485760 | tf_op jit(solution)/shard_map/reduce_scatter | solution.py:133
  190.2 15.6 %copy-start.3 = (f32[128,2048]{1,0:T(8,128)S(1)}, f32[128,2048]{1,0:T(8,128)}, u32[]{:S(2)}) copy-start(f32[128,2048]{1,0:T(8,128)} %rev.7) | copy-start | bytes 3145732
  205.8 51.7 %copy-start = (f32[512,1,2048]{2,0,1:T(8,128)S(1)}, f32[512,1,2048]{2,0,1:T(8,128)}, u32[]{:S(2)}) copy-start(f32[512,1,2048]{2,0,1:T(8,128)} %copy.99) | copy-start | bytes 12582916
  257.5 50.4 %copy-start.1 = (bf16[512,2048]{1,0:T(8,128)(2,1)S(1)}, bf16[512,2048]{1,0:T(8,128)(2,1)}, u32[]{:S(2)}) copy-start(bf16[512,2048]{1,0:T(8,128)(2,1)} %param.13) | copy-start | bytes 6291460
  260.3 47.7 %collective-permute-start.2 = (bf16[512,2048]{1,0:T(8,128)(2,1)}, bf16[512,2048]{1,0:T(8,128)(2,1)}, u32[]{:S(2)}, u32[]{:S(2)}) collective-permute-start(bf16[512,2048]{1,0:T(8,128)(2,1)} %fusion.37), channel_id=1, source_target_pairs={{0,8},{8,16},{16,24},{24,0},{1,9},{9,17},{17,25},{25,1},{2,10},{10... | collective-permute-start | bytes 6291464 | tf_op jit(solution)/shard_map/ppermute | solution.py:23
  260.3 58.2 %collective-permute-start.4 = (bf16[512,2048]{1,0:T(8,128)(2,1)}, bf16[512,2048]{1,0:T(8,128)(2,1)}, u32[]{:S(2)}, u32[]{:S(2)}) collective-permute-start(bf16[512,2048]{1,0:T(8,128)(2,1)} %fusion.37), channel_id=1, source_target_pairs={{8,0},{16,8},{24,16},{0,24},{9,1},{17,9},{25,17},{1,25},{10,2},{18... | collective-permute-start | bytes 6291464 | tf_op jit(solution)/shard_map/ppermute | solution.py:25
  307.9 25.8 %collective-permute-start.3 = (bf16[512,2048]{1,0:T(8,128)(2,1)}, bf16[512,2048]{1,0:T(8,128)(2,1)}, u32[]{:S(2)}, u32[]{:S(2)}) collective-permute-start(bf16[512,2048]{1,0:T(8,128)(2,1)} %collective-permute-done.2), channel_id=1, source_target_pairs={{0,8},{8,16},{16,24},{24,0},{1,9},{9,17},{17,25},{25,1},{2,10},{10... | collective-permute-start | bytes 6291464 | tf_op jit(solution)/shard_map/ppermute | solution.py:23
Sparse Core Ops, SparseCore 0:
  168.3 58.5 all-gather.1
  481.0 232.9 reduce-scatter.1
